TPU v7x, 128 devices: a whole 4x4x4 slice. The times are simulated.
128 devices in a mesh: tm: 64 (over z, x, y), blk: 2 (over core).
Axes of the slice: x: 4, y: 4, z: 4, core: 2. Of those that a mesh axis runs over, the one named last changes fastest.
Arguments:
- diag_blocks: float32 [128, 1024, 1024], P('tm', None, 'blk'), may hold values from -24 to 60, as said below
- sub_blocks: float32 [128, 1024, 1024], P('tm', None, 'blk'), may hold values from -17 to 2
- arrow_blocks: float32 [128, 64, 1024], P('tm', None, 'blk'), may hold values from -1 to 1
- tip_block: float32 [64, 64], replicated, may hold values from -2 to 14, as said below
Outputs:
- pivot_diag: float32 [64, 1024, 1024], P('tm', None, 'blk')
- pivot_left: float32 [64, 1024, 1024], P('tm', None, 'blk')
- pivot_arrow: float32 [64, 64, 1024], P('tm', None, 'blk')
- tip_schur: float32 [64, 64], replicated
- log_det: float32 [], replicated
Inputs may be any that keep to these rules, and one draw needn't show every extreme that they name: Every diag_blocks[s] is symmetric, and the slab part of Q (without the fixed-effect rows) is positive definite. tip_block is symmetric.
All inputs are finite; a program needn't handle non-finite values.
Results may differ from a plain program's by a relative error of at most 0.0003.
Values sent between devices are 32-bit elements; how exact they have to be, the bound alone decides.
A program may use at most 192 MiB of HBM per device.

v0:
```python
import functools

import jax
import jax.numpy as jnp
from jax import lax
from jax.experimental import pallas as pl
from jax.experimental.pallas import tpu as pltpu
from jax.sharding import PartitionSpec as P

F32 = jnp.float32
BF16 = jnp.bfloat16
TILE = 128
BLOCK = 256
PACKED = 5
COPIES = 4
SIDE = 4
GROUP = 2
SLOTS = TILE // (8 * GROUP)


def row_of(value, index):
    return jnp.broadcast_to(value[index : index + 1, :], (8, value.shape[1]))


def column_of(value, index):
    return jnp.broadcast_to(value[:, index : index + 1], (8, TILE))


def split_three(value):
    high = value.astype(BF16).astype(F32)
    rest = value - high
    middle = rest.astype(BF16).astype(F32)
    return high, middle, rest - middle


def split_two(value):
    high = value.astype(BF16)
    return high, (value - high.astype(F32)).astype(BF16)


def left_pieces(value):
    high, low = split_two(value)
    return jnp.concatenate([high, low, high], axis=1)


def right_pieces(value):
    high, low = split_two(value)
    return jnp.concatenate([high, high, low], axis=0)


def outer_product(rows_a, rows_b):
    ah, am, al = split_three(rows_a)
    bh, bm, bl = split_three(rows_b)
    left = jnp.concatenate([ah, am, ah, am, al, ah], axis=0).astype(BF16)
    right = jnp.concatenate([bh, bh, bm, bm, bh, bl], axis=0).astype(BF16)
    return lax.dot_general(left, right, (((0,), (0,)), ((), ())), preferred_element_type=F32)


def sweep_rows(rows, first, pivots, lane, sub):
    count = 8 * len(rows)
    columns = [[column_of(row, first + c) for c in range(count)] for row in rows]
    inside = (lane >= first) & (lane < first + count)
    solved = [
        jnp.where(lane == sub + first + 8 * h, -1.0, jnp.where(inside, 0.0, row)) for h, row in enumerate(rows)
    ]
    for c in range(count):
        group, place = c // 8, c % 8
        pivot = row_of(columns[group][c], place)
        scale = 1.0 / pivot
        pivots = jnp.where(lane == first + c, pivot, pivots)
        pivot_row = row_of(solved[group], place) * scale
        for h in range(len(rows)):
            value = solved[h] - columns[h][c] * pivot_row
            solved[h] = jnp.where(sub == place, pivot_row, value) if h == group else value
        for d in range(c + 1, count):
            entry = row_of(columns[group][d], place) * scale
            for h in range(len(rows)):
                value = columns[h][d] - columns[h][c] * entry
                columns[h][d] = jnp.where(sub == place, entry, value) if h == group else value
    return solved, pivots


def sweep_tile(tile, beside=None):
    lane = lax.broadcasted_iota(jnp.int32, (8, TILE), 1)
    sub = lax.broadcasted_iota(jnp.int32, (8, TILE), 0)
    pivots = jnp.ones((8, TILE), F32)
    width = 8 * GROUP
    rows = [tile[8 * i : 8 * i + 8, :] for i in range(TILE // 8)]
    for i in range(TILE // width):
        source = rows[GROUP * i : GROUP * i + GROUP]
        inside = (lane >= width * i) & (lane < width * i + width)
        solved, pivots = sweep_rows(source, width * i, pivots, lane, sub)
        update = outer_product(jnp.concatenate(source, axis=0), jnp.concatenate(solved, axis=0))
        for k in range(TILE // 8):
            if k // GROUP == i:
                continue
            kept = jnp.where(inside, 0.0, rows[k])
            if k == GROUP * (i + 1):
                for c in range(width):
                    kept = kept - column_of(rows[k], width * i + c) * row_of(solved[c // 8], c % 8)
                rows[k] = kept
            else:
                rows[k] = kept - update[8 * k : 8 * k + 8, :]
        rows[GROUP * i : GROUP * i + GROUP] = solved
        if beside is not None:
            beside(i)
    return jnp.concatenate(rows, axis=0), pivots


def tile_span(index):
    return pl.ds(pl.multiple_of(index * TILE, TILE), TILE)


def close_tile(order, matrix_ref, left_ref, swept_ref, tile_ref, j, swept):
    count = order // TILE
    here, there = tile_span(j), tile_span(lax.rem(j + 1, count))
    swept_ref[...] = swept
    solved = jnp.dot(left_pieces(swept), right_pieces(matrix_ref[here, there]), preferred_element_type=F32)
    tile_ref[...] = matrix_ref[there, there] + jnp.dot(
        left_pieces(matrix_ref[there, here]), right_pieces(solved), preferred_element_type=F32
    )
    matrix_ref[here, here] = jnp.zeros((TILE, TILE), F32)
    for r in range(count):
        span = slice(r * TILE, (r + 1) * TILE)
        left_ref[span, :] = left_pieces(matrix_ref[span, here])
    matrix_ref[:, here] = jnp.zeros((order, TILE), F32)
    matrix_ref[here, here] = swept


def solve_tile_rows(order, matrix_ref, swept_ref, right_ref, j):
    here = tile_span(j)
    rows = matrix_ref[here, :]
    lane = lax.broadcasted_iota(jnp.int32, (TILE, order), 1)
    inside = (lane >= j * TILE) & (lane < j * TILE + TILE)
    solved = -jnp.dot(left_pieces(swept_ref[...]), right_pieces(rows), preferred_element_type=F32)
    solved = jnp.where(inside, rows, solved)
    right_ref[...] = right_pieces(solved)
    matrix_ref[here, :] = solved


def update_rows(matrix_ref, left_ref, right_ref, span):
    matrix_ref[span, :] = matrix_ref[span, :] - jnp.dot(
        left_ref[span, :], right_ref[...], preferred_element_type=F32
    )


def eliminate_all(order, matrix_ref, log_ref, left_ref, right_ref, swept_ref, tile_ref):
    count = order // TILE
    swept, pivots = sweep_tile(matrix_ref[0:TILE, 0:TILE])
    close_tile(order, matrix_ref, left_ref, swept_ref, tile_ref, 0, swept)

    def step(j, logs):
        def beside(i):
            if i == 0:
                solve_tile_rows(order, matrix_ref, swept_ref, right_ref, j - 1)
                return
            first = (i - 1) * count // (SLOTS - 1)
            for r in range(first, i * count // (SLOTS - 1)):
                update_rows(matrix_ref, left_ref, right_ref, slice(r * TILE, (r + 1) * TILE))

        swept, pivots = sweep_tile(tile_ref[...], beside)
        close_tile(order, matrix_ref, left_ref, swept_ref, tile_ref, j, swept)
        return logs + jnp.log(pivots)

    log_ref[...] = lax.fori_loop(1, count, step, jnp.log(pivots))
    solve_tile_rows(order, matrix_ref, swept_ref, right_ref, count - 1)

    def update(r, carry):
        update_rows(matrix_ref, left_ref, right_ref, tile_span(r))
        return carry

    lax.fori_loop(0, count, update, 0)


def inverse_kernel(source_ref, inverse_ref, log_ref, *scratch):
    order = source_ref.shape[0]

    def take(r, carry):
        inverse_ref[tile_span(r), :] = source_ref[tile_span(r), :]
        return carry

    lax.fori_loop(0, order // TILE, take, 0)
    eliminate_all(order, inverse_ref, log_ref, *scratch)


def packed_inverse_kernel(info_ref, both_ref, inverse_ref, log_ref, own_ref, *scratch):
    order, half = own_ref.shape
    places = (((0, 0), (1, 0), (2, 0), (1, 1), (2, 1)), ((0, 3), (1, 3), (2, 3), (3, 3), (2, 2)))
    for source in range(2):
        for k, (row, column) in enumerate(places[source]):
            value = both_ref[source, k * BLOCK : (k + 1) * BLOCK, :]
            rows = slice(row * BLOCK, (row + 1) * BLOCK)
            columns = slice(column * BLOCK, (column + 1) * BLOCK)
            inverse_ref[rows, columns] = value
            if row != column:
                inverse_ref[columns, rows] = value.T
    own = pl.ds(pl.multiple_of(info_ref[0] * half, half), half)
    own_ref[...] = inverse_ref[:, own]
    eliminate_all(order, inverse_ref, log_ref, *scratch)


def inverse_scratch(order):
    return [
        pltpu.VMEM((order, 3 * TILE), BF16),
        pltpu.VMEM((3 * TILE, order), BF16),
        pltpu.VMEM((TILE, TILE), F32),
        pltpu.VMEM((TILE, TILE), F32),
    ]


def inverse_and_log(matrix):
    order = matrix.shape[0]
    return local_call(
        inverse_kernel, "first_inverse", 24 * order**3, 16,
        out_shape=[shape_of(order, order), shape_of(8, TILE)],
        in_specs=vmem(1), out_specs=vmem(2), scratch_shapes=inverse_scratch(order),
    )(matrix)


def inverse_of_packed(info, both, order, half):
    return local_call(
        packed_inverse_kernel, "second_inverse", 24 * order**3, 20,
        out_shape=[shape_of(order, order), shape_of(8, TILE), shape_of(order, half)],
        in_specs=[SMEM_SPEC, *vmem(1)], out_specs=vmem(3), scratch_shapes=inverse_scratch(order),
    )(info, both)


def times(left, right, left_dim=1, right_dim=0):
    dims = (((left_dim,), (right_dim,)), ((), ()))

    def dot(a, b):
        return lax.dot_general(a, b, dims, preferred_element_type=F32)

    return dot(left[0], right[0]) + (dot(left[0], right[1]) + dot(left[1], right[0]))


def split_rows(source, high_ref, low_ref, sign=1):
    def part(r, carry):
        high, low = split_two(sign * source[tile_span(r), :])
        high_ref[tile_span(r), :] = high
        low_ref[tile_span(r), :] = low
        return carry

    lax.fori_loop(0, high_ref.shape[0] // TILE, part, 0)


def block_span(index):
    return pl.ds(pl.multiple_of(index * BLOCK, BLOCK), BLOCK)


def packed_place(core, k):
    row = jnp.where(core == 0, jnp.where(k < 3, k, k - 2), jnp.where(k < 4, k, 2))
    column = jnp.where(core == 0, jnp.where(k < 3, 0, 1), jnp.where(k < 4, 1, 0))
    return row, column


def solve_into(inverse, right, out, right_dim):
    def part(r, carry):
        rows = block_span(r)
        value = times((inverse[0][rows, :], inverse[1][rows, :]), right, 1, right_dim)
        out[0][rows, :], out[1][rows, :] = split_two(value)
        return carry

    lax.fori_loop(0, inverse[0].shape[0] // BLOCK, part, 0)


def packed_gram(core, former, solved, left_dim, store):
    def part(k, carry):
        row, column = packed_place(core, k)
        if left_dim == 0:
            left = (former[0][:, block_span(row)], former[1][:, block_span(row)])
        else:
            left = (former[0][block_span(row), :], former[1][block_span(row), :])
        right = (solved[0][:, block_span(column)], solved[1][:, block_span(column)])
        store(k, row, column, times(left, right, left_dim, 0))
        return carry

    lax.fori_loop(0, PACKED, part, 0)


def arrow_pack(value):
    return jnp.concatenate([value[:, :BLOCK], value[:, BLOCK:]], axis=0)


def arrow_unpack(value):
    effects = value.shape[0] // 2
    return jnp.concatenate([value[:effects], value[effects:]], axis=1)


def fetch(pairs, sems):
    copies = [pltpu.make_async_copy(source, target, sems.at[k]) for k, (source, target) in enumerate(pairs)]
    for copy in copies:
        copy.start()
    return copies


def arrow_form(rows, inverse_ref):
    pieces = split_two(rows)
    through = -times(pieces, split_two(inverse_ref[...]))
    return times(split_two(through), pieces, 1, 1)


def separator_arrow(packed):
    return jnp.concatenate([arrow_unpack(packed[0]), arrow_unpack(packed[1])], axis=1)


def second_products_kernel(
    info_ref, inverse_hbm, left_hbm, both_hbm, rest_hbm, out_ref,
    inverse_ref, left_ref, arrow_ref, rest_ref, sems, vh, vl, bh, bl, xh, xl,
):
    core, even = info_ref[0], info_ref[1] == 1
    half = xh.shape[1]
    own = pl.ds(pl.multiple_of(core * half, half), half)
    last = slice(PACKED * BLOCK, None)
    copies = fetch(
        (
            (inverse_hbm, inverse_ref),
            (left_hbm, left_ref),
            (both_hbm.at[:, pl.ds(PACKED * BLOCK, arrow_ref.shape[1]), :], arrow_ref),
            (rest_hbm, rest_ref),
        ),
        sems,
    )
    copies[0].wait()
    split_rows(inverse_ref, vh, vl, -1)
    copies[1].wait()
    split_rows(left_ref, bh, bl)
    for copy in copies[2:]:
        copy.wait()
    rows = split_two(separator_arrow(arrow_ref[...]))

    @pl.when(even)
    def _():
        solve_into((vh, vl), (bh[:, own], bl[:, own]), (xh, xl), 0)

        def store(k, row, column, value):
            out_ref[block_span(k), :] = rest_ref[block_span(k), :] + value

        packed_gram(core, (bh, bl), (xh, xl), 0, store)
        out_ref[last, :] = rest_ref[last, :] + arrow_pack(times(rows, (xh[...], xl[...])))

    @pl.when(jnp.logical_not(even))
    def _():
        solve_into((vh, vl), (bh[own, :], bl[own, :]), (xh, xl), 1)

        def store(k, row, column, value):
            span = block_span(k)
            out_ref[span, :] = rest_ref[span, :] - value

        packed_gram(core, (bh, bl), (xh, xl), 1, store)
        change = arrow_pack(times(rows, (xh[...], xl[...])))
        out_ref[last, :] = rest_ref[last, :] - change


def second_terms_kernel(info_ref, inverse_hbm, arrow_ref, pair_sums_ref, log_ref, sums_ref, inverse_ref, sem):
    sums_ref[...] = pair_sums_ref[...]

    @pl.when(info_ref[1] == 0)
    def _():
        copy = pltpu.make_async_copy(inverse_hbm, inverse_ref, sem)
        copy.start()
        copy.wait()
        put_sums(sums_ref, arrow_form(separator_arrow(arrow_ref[...]), inverse_ref), log_ref[...])
        sums_ref[...] = sums_ref[...] + pair_sums_ref[...]


def second_fill_kernel(
    info_ref, totals_ref, inverse_hbm, left_hbm, own_hbm, pair_hbm, out_ref,
    inverse_ref, left_ref, pair_ref, sems, vh, vl, bh, bl, xh, xl,
):
    even = info_ref[1] == 1

    @pl.when(even)
    def _():
        copy = pltpu.make_async_copy(own_hbm, out_ref.at[0], sems.at[0])
        copy.start()
        copy.wait()

    @pl.when(jnp.logical_not(even))
    def _():
        copies = fetch(((inverse_hbm, inverse_ref), (pair_hbm, pair_ref), (left_hbm, left_ref)), sems)
        copies[0].wait()
        split_rows(inverse_ref, vh, vl, -1)
        copies[1].wait()
        solve_into((vh, vl), split_two(pair_ref[...]), (xh, xl), 0)
        copies[2].wait()
        split_rows(left_ref, bh, bl)

        def part(r, carry):
            rows = block_span(r)
            out_ref[0, rows, :] = -times((bh[rows, :], bl[rows, :]), (xh[...], xl[...]))
            return carry

        lax.fori_loop(0, bh.shape[0] // BLOCK, part, 0)


def meet(devices):
    barrier = pltpu.get_barrier_semaphore()
    for device in devices:
        pl.semaphore_signal(barrier, inc=1, device_id=device, device_id_type=pl.DeviceIdType.MESH)
    pl.semaphore_wait(barrier, len(devices))


def exchange(parts, peer, send_sem, recv_sem):
    copies = []
    for k, (source, target) in enumerate(parts):
        copies.append(
            pltpu.make_async_remote_copy(
                src_ref=source,
                dst_ref=target,
                send_sem=send_sem.at[k],
                recv_sem=recv_sem.at[k],
                device_id=peer,
                device_id_type=pl.DeviceIdType.MESH,
            )
        )
        copies[-1].start()
    return copies


def gather_kernel(diag_ref, arrow_ref, out_ref, arrow_out_ref, local_sems, send_sem, recv_sem):
    core = lax.axis_index("blk")
    peer = {"blk": 1 - core}
    half = diag_ref.shape[2]
    rows = diag_ref.shape[1] // COPIES
    own = pl.ds(pl.multiple_of(core * half, half), half)
    local = pltpu.make_async_copy(diag_ref.at[0], out_ref.at[:, own], local_sems.at[0])
    local.start()
    local_arrow = pltpu.make_async_copy(arrow_ref.at[0], arrow_out_ref.at[0, :, own], local_sems.at[1])
    local_arrow.start()
    meet([peer])
    spans = [pl.ds(k * rows, rows) for k in range(COPIES)]
    parts = [(diag_ref.at[0, span, :], out_ref.at[span, own]) for span in spans]
    parts.append((arrow_ref.at[0], arrow_out_ref.at[0, :, own]))
    copies = exchange(parts, peer, send_sem, recv_sem)
    local.wait()
    local_arrow.wait()
    for copy in copies:
        copy.wait()


def put_sums(sums_ref, tip, logs):
    effects = tip.shape[0]
    sums_ref[...] = jnp.zeros_like(sums_ref)
    sums_ref[0:effects, 0:effects] = tip
    sums_ref[effects:, :] = logs


def pair_kernel(
    inverse_hbm, sub_hbm, diag_hbm, own_arrow_hbm, arrow_ref, log_ref,
    both_hbm, left_out_ref, rest_ref, pair_sums_ref,
    inverse_ref, left_ref, right_ref, diag_ref, own_arrow_ref, swap_ref, other_ref, sum_ref,
    own_sums_ref, other_sums_ref, vh, vl, bh, bl, sh, sl, xh, xl, yh, yl,
    sems, local_sems, swap_send, swap_recv, send_sem, recv_sem, sums_send, sums_recv,
):
    core, me = lax.axis_index("blk"), lax.axis_index("tm")
    even = me % 2 == 0
    peer, partner = {"blk": 1 - core}, {"tm": me + 1 - 2 * (me % 2)}
    half = diag_ref.shape[1]
    own = pl.ds(pl.multiple_of(core * half, half), half)
    copies = fetch(
        (
            (inverse_hbm, inverse_ref),
            (sub_hbm.at[0], left_ref),
            (sub_hbm.at[1], right_ref),
            (diag_hbm.at[1], diag_ref),
            (own_arrow_hbm.at[1], own_arrow_ref),
        ),
        sems,
    )
    copies[0].wait()
    split_rows(inverse_ref, vh, vl, -1)
    copies[1].wait()
    split_rows(left_ref, bh, bl)
    solve_into((vh, vl), (bh[:, own], bl[:, own]), (xh, xl), 0)
    copies[2].wait()
    split_rows(right_ref, sh, sl)
    solve_into((vh, vl), (sh[own, :], sl[own, :]), (yh, yl), 1)
    copies[3].wait()
    copies[4].wait()
    meet([peer, partner])

    def keep(span, lower, upper):
        swap_ref[span, :] = jnp.where(even, upper, lower)
        rest_ref[span, :] = jnp.where(even, lower, upper)

    def swap(span, k):
        return pltpu.make_async_remote_copy(
            src_ref=swap_ref.at[span, :],
            dst_ref=other_ref.at[span, :],
            send_sem=swap_send.at[k],
            recv_sem=swap_recv.at[k],
            device_id=partner,
            device_id_type=pl.DeviceIdType.MESH,
        )

    def blocks(k, carry):
        row, column = packed_place(core, k)
        rows, columns = block_span(row), block_span(column)
        lower = times((bh[:, rows], bl[:, rows]), (xh[:, columns], xl[:, columns]), 0, 0)
        change = times((sh[rows, :], sl[rows, :]), (yh[:, columns], yl[:, columns]))
        keep(block_span(k), lower, diag_ref[rows, columns] - change)
        swap(block_span(k), k).start()
        return carry

    lax.fori_loop(0, PACKED, blocks, 0)
    rows = split_two(arrow_ref[0])
    last = pl.ds(PACKED * BLOCK, swap_ref.shape[0] - PACKED * BLOCK)
    keep(
        last,
        arrow_pack(times(rows, (xh[...], xl[...]))),
        arrow_pack(own_arrow_ref[...] - times(rows, (yh[...], yl[...]))),
    )
    swap(last, PACKED).start()

    def part(r, carry):
        span = block_span(r)
        value = -times((sh[span, :], sl[span, :]), (xh[...], xl[...]))
        left_out_ref[span, :] = jnp.where(me > 0, value, 0.0)
        return carry

    lax.fori_loop(0, sh.shape[0] // BLOCK, part, 0)
    put_sums(own_sums_ref, arrow_form(arrow_ref[0], inverse_ref), log_ref[...])
    sums = exchange([(own_sums_ref, other_sums_ref)], partner, sums_send, sums_recv)
    shares = []
    for k in range(PACKED + 1):
        span = last if k == PACKED else pl.ds(k * BLOCK, BLOCK)
        swap(span, k).wait()
        difference = swap_ref[span, :] - other_ref[span, :]
        sum_ref[span, :] = jnp.where(even, difference, -difference)
        local = pltpu.make_async_copy(sum_ref.at[span, :], both_hbm.at[core, span, :], local_sems.at[k])
        local.start()
        shares.append(local)
        shares += exchange(
            [(sum_ref.at[span, :], both_hbm.at[core, span, :])], peer, send_sem.at[pl.ds(k, 1)], recv_sem.at[pl.ds(k, 1)]
        )
    for copy in shares + sums:
        copy.wait()
    pair_sums_ref[...] = own_sums_ref[...] + other_sums_ref[...]


def finish_kernel(kept_ref, above_ref, out_ref, peer_ref, send_sem, recv_sem):
    core = lax.axis_index("blk")
    peer = {"blk": 1 - core}
    out_ref[...] = kept_ref[...] - above_ref[...]
    meet([peer])
    copies = []
    for slot, block in enumerate((2 - 2 * core, 4 - 3 * core)):
        copies.append(
            pltpu.make_async_remote_copy(
                src_ref=out_ref.at[block_span(block), :],
                dst_ref=peer_ref.at[pl.ds(slot * BLOCK, BLOCK), :],
                send_sem=send_sem.at[slot],
                recv_sem=recv_sem.at[slot],
                device_id=peer,
                device_id_type=pl.DeviceIdType.MESH,
            )
        )
        copies[-1].start()
    for copy in copies:
        copy.wait()


def place_kernel(info_ref, packed_ref, peer_ref, separator_ref, out_ref):
    core, even = info_ref[0], info_ref[1] == 1

    @pl.when(even)
    def _():
        out_ref[0] = separator_ref[...]

    def packed(k):
        return packed_ref[k * BLOCK : (k + 1) * BLOCK, :]

    def put(row, column, value):
        out_ref[0, row * BLOCK : (row + 1) * BLOCK, column * BLOCK : (column + 1) * BLOCK] = value

    first, second = peer_ref[:BLOCK, :], peer_ref[BLOCK:, :]
    odd = jnp.logical_not(even)

    @pl.when(odd & (core == 0))
    def _():
        for row, column, value in (
            (0, 0, packed(0)), (1, 0, packed(1)), (2, 0, packed(2)), (3, 0, first.T),
            (0, 1, packed(1).T), (1, 1, packed(3)), (2, 1, packed(4)), (3, 1, second.T),
        ):
            put(row, column, value)

    @pl.when(odd & (core == 1))
    def _():
        for row, column, value in (
            (0, 0, first.T), (1, 0, second.T), (2, 0, packed(4)), (3, 0, packed(2).T),
            (0, 1, packed(0)), (1, 1, packed(1)), (2, 1, packed(2)), (3, 1, packed(3)),
        ):
            put(row, column, value)


def reduce_kernel(side, value_ref, out_ref, parts_ref, first_sems, send_sem, recv_sem, last_send, last_recv):
    me = lax.axis_index("tm")
    place_y = me % side
    root = me - place_y + 1
    stages = [((me // side) % side, side), ((me // side**2) % side, side**2)]

    def other(stage, step):
        place, stride = stages[stage]
        return me + ((place + step) % side - place) * stride

    def hand(source, target, send, recv, device):
        return pltpu.make_async_remote_copy(
            src_ref=source,
            dst_ref=target,
            send_sem=send,
            recv_sem=recv,
            device_id={"tm": device},
            device_id_type=pl.DeviceIdType.MESH,
        )

    slot = parts_ref.at[len(stages), 0]

    @pl.when(place_y == 1)
    def _():
        row = (me - 1, me + 1, me + 2)
        meet([{"tm": other(s, d)} for s in range(len(stages)) for d in range(1, side)] + [{"tm": k} for k in row])
        hand(value_ref, slot, first_sems.at[0], first_sems.at[1], me + 2).wait_recv()
        out_ref[...] = value_ref[...] + parts_ref[len(stages), 0]
        for s, (place, _) in enumerate(stages):
            parts_ref[s, place] = out_ref[...]
            copies = []
            for d in range(1, side):
                copies += exchange(
                    [(out_ref, parts_ref.at[s, place])],
                    {"tm": other(s, d)},
                    send_sem.at[s, pl.ds(d, 1)],
                    recv_sem.at[s, pl.ds(d, 1)],
                )
            for copy in copies:
                copy.wait()
            total = parts_ref[s, 0]
            for k in range(1, side):
                total = total + parts_ref[s, k]
            out_ref[...] = total
        copies = [hand(out_ref, out_ref, last_send.at[k], last_recv, device) for k, device in enumerate(row)]
        for copy in copies:
            copy.start()
        for copy in copies:
            copy.wait_send()

    @pl.when(place_y != 1)
    def _():
        meet([{"tm": root}])

        @pl.when(place_y == 3)
        def _():
            copy = hand(value_ref, slot, first_sems.at[0], first_sems.at[1], root)
            copy.start()
            copy.wait_send()

        hand(out_ref, out_ref, last_send.at[0], last_recv, root).wait_recv()


def vmem(count):
    return [pl.BlockSpec(memory_space=pltpu.VMEM)] * count


def shape_of(*sizes, dtype=F32):
    return jax.ShapeDtypeStruct(sizes, dtype)


SMEM_SPEC = pl.BlockSpec(memory_space=pltpu.SMEM)
ANY_SPEC = pl.BlockSpec(memory_space=pl.ANY)
HBM_SPEC = pl.BlockSpec(memory_space=pltpu.HBM)


def local_call(kernel, name, flops, mebibytes, **kwargs):
    return pl.pallas_call(
        kernel,
        compiler_params=pltpu.CompilerParams(vmem_limit_bytes=mebibytes * 2**20),
        cost_estimate=pl.CostEstimate(flops=flops, bytes_accessed=2**23, transcendentals=0),
        name=name,
        **kwargs,
    )


def remote_call(kernel, name, identity, mebibytes=24, **kwargs):
    return pl.pallas_call(
        kernel,
        compiler_params=pltpu.CompilerParams(
            collective_id=identity, has_side_effects=True, vmem_limit_bytes=mebibytes * 2**20
        ),
        name=name,
        **kwargs,
    )


def dma_sems(*shape):
    return pltpu.SemaphoreType.DMA(shape)


def whole(shape, index):
    return pl.BlockSpec(shape, lambda i: index, pipeline_mode=pl.Buffered(1))


def on_device(diag_blocks, sub_blocks, arrow_blocks, tip_block):
    partition = lax.axis_index("tm")
    parts = lax.axis_size("tm")
    order, half = diag_blocks.shape[1:]
    effects = arrow_blocks.shape[1]
    packed_rows = PACKED * BLOCK + effects * half // BLOCK
    evens = range(0, parts, 2)
    down = [(p, p - 1) for p in evens if p > 0]
    core = lax.axis_index("blk")
    info = jnp.stack([core, (partition % 2 == 0).astype(core.dtype), (partition > 0).astype(core.dtype)])
    square, tall = (order, order), (order, half)
    big = [pltpu.VMEM(square, BF16)] * 2
    thin = [pltpu.VMEM(tall, BF16)] * 2

    pivot, arrow_full = remote_call(
        gather_kernel, "gather_pivot", 1,
        out_shape=[shape_of(*square), shape_of(1, effects, order)],
        in_specs=[HBM_SPEC] * 2, out_specs=[ANY_SPEC] * 2,
        scratch_shapes=[dma_sems(2), dma_sems(COPIES + 1), dma_sems(COPIES + 1)],
    )(diag_blocks, arrow_blocks)
    sub_full = lax.all_gather(sub_blocks, "blk", axis=2, tiled=True)
    inverse, log_first = inverse_and_log(pivot)

    packed_shape = shape_of(packed_rows, BLOCK)
    packed_scratch = pltpu.VMEM((packed_rows, BLOCK), F32)
    pairs = [(p, p + 1) for p in evens]
    both, left_own, rest, pair_sums = remote_call(
        pair_kernel, "products_and_swap", 2, 58,
        out_shape=[shape_of(2, packed_rows, BLOCK), shape_of(*tall), packed_shape, shape_of(effects + 8, TILE)],
        in_specs=[*[ANY_SPEC] * 4, *vmem(2)],
        out_specs=[ANY_SPEC, *vmem(3)],
        scratch_shapes=[pltpu.VMEM(square, F32)] * 3
        + [pltpu.VMEM(tall, F32), pltpu.VMEM((effects, half), F32)]
        + [packed_scratch] * 3
        + [pltpu.VMEM((effects + 8, TILE), F32)] * 2
        + big * 3
        + thin * 2
        + [dma_sems(5), *[dma_sems(PACKED + 1)] * 5, dma_sems(1), dma_sems(1)],
    )(inverse, sub_full, diag_blocks, arrow_blocks, arrow_full, log_first)
    left_pair = lax.ppermute(left_own, "tm", pairs)
    left_full = lax.all_gather(left_own, "blk", axis=1, tiled=True)

    inverse, log_second, separator = inverse_of_packed(info, both, order, half)
    product = local_call(
        second_products_kernel, "second_products", 5 * order**3, 58,
        out_shape=packed_shape,
        in_specs=[SMEM_SPEC, *[ANY_SPEC] * 4],
        out_specs=vmem(1)[0],
        scratch_shapes=[pltpu.VMEM(square, F32)] * 2
        + [pltpu.VMEM((2, packed_rows - PACKED * BLOCK, BLOCK), F32), packed_scratch, dma_sems(4)]
        + big * 2
        + thin,
    )(info, inverse, left_full, both, rest)
    above = lax.ppermute(product, "tm", down)
    sums = local_call(
        second_terms_kernel, "second_terms", order**3 // 2, 24,
        out_shape=shape_of(effects + 8, TILE),
        in_specs=[SMEM_SPEC, ANY_SPEC, *vmem(3)],
        out_specs=vmem(1)[0],
        scratch_shapes=[pltpu.VMEM(square, F32), pltpu.SemaphoreType.DMA],
    )(info, inverse, both[:, PACKED * BLOCK :], pair_sums, log_second)
    totals = remote_call(
        functools.partial(reduce_kernel, SIDE), "reduce_terms", 3,
        out_shape=shape_of(effects + 8, TILE), in_specs=vmem(1), out_specs=vmem(1)[0],
        scratch_shapes=[
            pltpu.VMEM((3, SIDE, effects + 8, TILE), F32),
            dma_sems(2), dma_sems(2, SIDE), dma_sems(2, SIDE), dma_sems(3), pltpu.SemaphoreType.DMA,
        ],
    )(sums)
    left_result = local_call(
        second_fill_kernel, "second_fill", 6 * order**3, 58,
        out_shape=shape_of(1, *tall),
        in_specs=[SMEM_SPEC, *vmem(1), *[ANY_SPEC] * 4],
        out_specs=vmem(1)[0],
        scratch_shapes=[pltpu.VMEM(square, F32)] * 2 + [pltpu.VMEM(tall, F32), dma_sems(3)] + big * 2 + thin,
    )(info, totals, inverse, left_full, left_own, left_pair)
    packed, swapped = remote_call(
        finish_kernel, "finish_blocks", 4,
        out_shape=[packed_shape, shape_of(2 * BLOCK, BLOCK)], in_specs=vmem(2), out_specs=vmem(2),
        scratch_shapes=[dma_sems(2), dma_sems(2)],
    )(product, above)
    diag_result = local_call(
        place_kernel, "place_blocks", 2**20, 12,
        out_shape=shape_of(1, *tall), in_specs=[SMEM_SPEC, *vmem(3)], out_specs=vmem(1)[0],
    )(info, packed, swapped, separator)
    last = PACKED * BLOCK
    own_arrow = lax.dynamic_index_in_dim(both[:, last:], core, 0, keepdims=False)
    arrow_result = arrow_unpack(jnp.where(info[1] == 1, own_arrow, packed[last:]))
    return (
        diag_result,
        left_result,
        arrow_result[None],
        tip_block - totals[:effects, :effects],
        jnp.sum(totals[effects]),
    )


def solution(mesh):
    in_specs = (P("tm", None, "blk"), P("tm", None, "blk"), P("tm", None, "blk"), P())
    out_specs = (P("tm", None, "blk"), P("tm", None, "blk"), P("tm", None, "blk"), P(), P())
    return jax.shard_map(
        on_device, mesh=mesh, in_specs=in_specs, out_specs=out_specs, check_vma=False
    )
```

profile of v0, /device:TPU:25, one launch (start us, length us, event | category | flops | bytes accessed | tf_op | source)
XLA Modules:
  0.0 216.1 jit_solution(17326440467296619196)
XLA Ops:
  7.2 0.7 all-gather.3.cloned.1.call-update
  8.1 2.2 %copy-done = f32[2,1024,512]{2,1,0:T(8,128)S(1)} copy-done((f32[2,1024,512]{2,1,0:T(8,128)S(1)}, f32[2,1024,512]{2,1,0:T(8,128)}, u32[]{:S(2)}) %copy-start) | copy-done | bytes 4194328
  10.3 5.2 %gather_pivot.1 = (f32[1024,1024]{1,0:T(8,128)S(1)}, f32[1,64,1024]{2,1,0:T(8,128)S(1)}) custom-call(f32[2,1024,512]{2,1,0:T(8,128)S(1)} %copy-done, f32[2,64,512]{2,1,0:T(8,128)S(1)} %copy-done.5), custom_call_target="tpu_custom_call" | custom-call | tf_op jit(solution)/shard_map/gather_pivot/pallas_call | solution.py:716
  15.5 0.7 copy-done.6
  16.2 33.8 %first_inverse.1 = (f32[1024,1024]{1,0:T(8,128)S(1)}, f32[8,128]{1,0:T(8,128)S(1)}) custom-call(f32[1024,1024]{1,0:T(8,128)S(1)} %get-tuple-element.18.source_ref), custom_call_target="tpu_custom_call" | custom-call | flops 25769803776 | bytes 8388608 | tf_op jit(solution)/shard_map/first_inverse/pallas_call | solution.py:213
  50.0 2.0 copy-done.1
  51.9 0.6 copy-done.13
  52.5 52.9 %products_and_swap.1 = (f32[2,1408,256]{2,1,0:T(8,128)}, f32[1024,512]{1,0:T(8,128)}, f32[1408,256]{1,0:T(8,128)}, f32[72,128]{1,0:T(8,128)}) custom-call(f32[1024,1024]{1,0:T(8,128)} %copy-done.1, f32[2,1024,1024]{2,1,0:T(8,128)} %all-gather.3.cloned.1.call-done.sub_hbm, f32[2,1024,512]{2,1,0:T(8,128)} %diag_hbm.1, f32[2,64,512]{2,1,0:T(8,128)} %own_arrow_hbm.1, ...), custom_call_target="tpu_custom_call" | custom-call | tf_op jit(solution)/shard_map/products_and_swap/pallas_call | solution.py:728
  105.6 1.5 collective-permute-start.1
  107.1 1.8 copy-done.9
  108.9 34.1 %second_inverse.1 = (f32[1024,1024]{1,0:T(8,128)S(1)}, f32[8,128]{1,0:T(8,128)S(1)}, f32[1024,512]{1,0:T(8,128)S(1)}) custom-call(s32[3]{0:T(128)S(1)} %pad_add_fusion.info_ref, f32[2,1408,256]{2,1,0:T(8,128)S(1)} %copy-done.9), custom_call_target="tpu_custom_call" | custom-call | flops 25769803776 | bytes 8388608 | tf_op jit(solution)/shard_map/second_inverse/pallas_call | solution.py:221
  143.0 2.0 copy-done.2
  145.0 13.8 %second_products.1.kept_ref = f32[1408,256]{1,0:T(8,128)} custom-call(s32[3]{0:T(128)} %copy-done.10, f32[1024,1024]{1,0:T(8,128)} %copy-done.2, f32[1024,1024]{1,0:T(8,128)} %all-gather.5.cloned.1.call-done.left_hbm, f32[2,1408,256]{2,1,0:T(8,128)} %get-tuple-element.22.both_ref.both_hbm, f32[1408,256]{1,0:T(8,128)} %get-tuple-element.25.rest_hbm), custom_call_target="tpu_custom_call" | custom-call | flops 5368709120 | bytes 8388608 | tf_op jit(solution)/shard_map/second_products/pallas_call | solution.py:745
  158.9 1.3 collective-permute-start
  160.2 1.0 slice.19.arrow_ref
  161.2 2.2 %copy-done.3 = f32[1024,1024]{1,0:T(8,128)S(1)} copy-done((f32[1024,1024]{1,0:T(8,128)S(1)}, f32[1024,1024]{1,0:T(8,128)}, u32[]{:S(2)}) %copy-start.3) | copy-done | bytes 4194328
  163.4 2.4 %second_terms.1.value_ref = f32[72,128]{1,0:T(8,128)S(1)} custom-call(s32[3]{0:T(128)S(1)} %copy-done.11, f32[1024,1024]{1,0:T(8,128)S(1)} %copy-done.3, f32[2,128,256]{2,1,0:T(8,128)S(1)} %slice.19.arrow_ref, f32[72,128]{1,0:T(8,128)S(1)} %copy-done.8, f32[8,128]{1,0:T(8,128)S(1)} %get-tuple-element.30.log_ref), custom_call_target="tpu_custom_call" | custom-call | flops 536870912 | bytes 8388608 | tf_op jit(solution)/shard_map/second_terms/pallas_call | solution.py:756
  165.8 17.9 %reduce_terms.1.totals_ref = f32[72,128]{1,0:T(8,128)S(1)} custom-call(f32[72,128]{1,0:T(8,128)S(1)} %second_terms.1.value_ref), custom_call_target="tpu_custom_call" | custom-call | tf_op jit(solution)/shard_map/reduce_terms/pallas_call | solution.py:763
  183.7 0.6 slice_reduce_fusion
  184.3 0.6 slice_subtract_fusion
  185.0 14.3 %second_fill.1 = f32[1,1024,512]{2,1,0:T(8,128)} custom-call(s32[3]{0:T(128)} %copy-done.10, f32[72,128]{1,0:T(8,128)} %copy-done.7, f32[1024,1024]{1,0:T(8,128)} %copy-done.2, f32[1024,1024]{1,0:T(8,128)} %all-gather.5.cloned.1.call-done.left_hbm, f32[1024,512]{1,0:T(8,128)} %get-tuple-element.24.own_hbm, f32[1024,512]{1,0:T(8,128)} %collective-permute-done.1.pair_hbm), custom_call_target="tpu_custom_call" | custom-call | flops 6442450944 | bytes 8388608 | tf_op jit(solution)/shard_map/second_fill/pallas_call | solution.py:771
  199.3 7.0 %finish_blocks.1 = (f32[1408,256]{1,0:T(8,128)S(1)}, f32[512,256]{1,0:T(8,128)S(1)}) custom-call(f32[1408,256]{1,0:T(8,128)S(1)} %copy-done.4, f32[1408,256]{1,0:T(8,128)} %collective-permute-done.above_ref), custom_call_target="tpu_custom_call" | custom-call | tf_op jit(solution)/shard_map/finish_blocks/pallas_call | solution.py:778
  206.4 0.7 maximum_bitcast_fusion
  207.1 2.2 %place_blocks.1 = f32[1,1024,512]{2,1,0:T(8,128)} custom-call(s32[3]{0:T(128)S(1)} %copy-done.12, f32[1408,256]{1,0:T(8,128)S(1)} %get-tuple-element.26.packed_ref, f32[512,256]{1,0:T(8,128)S(1)} %get-tuple-element.27.peer_ref, f32[1024,512]{1,0:T(8,128)S(1)} %get-tuple-element.28.separator_ref), custom_call_target="tpu_custom_call" | custom-call | flops 1048576 | bytes 8388608 | tf_op jit(solution)/shard_map/place_blocks/pallas_call | solution.py:783
  (33 shorter events, 0.4 us)
Async XLA Ops:
  7.2 1.0 copy-start.5
  7.2 45.4 %all-gather.3.cloned.1.call-start = ((), (), s32[]{:S(2)}) async-start(), calls=%async_computation | async-start | bytes 12582912 | tf_op jit(solution)/shard_map/all_gather | solution.py:722
  7.9 137.1 %all-gather.5.cloned.1.call-start = ((), (), s32[]{:S(2)}) async-start(), calls=%async_computation.1 | async-start | bytes 6291456 | tf_op jit(solution)/shard_map/all_gather | solution.py:742
  8.1 2.2 %copy-start = (f32[2,1024,512]{2,1,0:T(8,128)S(1)}, f32[2,1024,512]{2,1,0:T(8,128)}, u32[]{:S(2)}) copy-start(f32[2,1024,512]{2,1,0:T(8,128)} %diag_hbm.1) | copy-start | bytes 12582916
  15.5 0.7 copy-start.6
  50.0 2.0 copy-start.1
  51.9 0.6 copy-start.13
  105.6 37.4 %copy-start.10 = (s32[3]{0:T(128)}, s32[3]{0:T(128)S(1)}, u32[]{:S(2)}) copy-start(s32[3]{0:T(128)S(1)} %pad_add_fusion.info_ref) | copy-start | bytes 40
  105.6 79.4 %collective-permute-start.1 = (f32[1024,512]{1,0:T(8,128)}, f32[1024,512]{1,0:T(8,128)}, u32[]{:S(2)}, u32[]{:S(2)}) collective-permute-start(f32[1024,512]{1,0:T(8,128)} %get-tuple-element.24.own_hbm), channel_id=1, source_target_pairs={{0,2},{4,6},{8,10},{12,14},{16,18},{20,22},{24,26},{28,30},{32,34}... | collective-permute-start | bytes 6291464 | tf_op jit(solution)/shard_map/ppermute | solution.py:741
  107.1 1.8 copy-start.9
  143.0 2.0 copy-start.2
  145.0 16.1 %copy-start.8 = (f32[72,128]{1,0:T(8,128)S(1)}, f32[72,128]{1,0:T(8,128)}, u32[]{:S(2)}) copy-start(f32[72,128]{1,0:T(8,128)} %get-tuple-element.29.pair_sums_ref) | copy-start | bytes 110596
  145.0 16.1 %copy-start.11 = (s32[3]{0:T(128)S(1)}, s32[3]{0:T(128)}, u32[]{:S(2)}) copy-start(s32[3]{0:T(128)} %copy-done.10) | copy-start | bytes 40
  158.9 40.4 %collective-permute-start = (f32[1408,256]{1,0:T(8,128)}, f32[1408,256]{1,0:T(8,128)}, u32[]{:S(2)}, u32[]{:S(2)}) collective-permute-start(f32[1408,256]{1,0:T(8,128)} %second_products.1.kept_ref), channel_id=1, source_target_pairs={{4,2},{8,6},{12,10},{16,14},{20,18},{24,22},{28,26},{32,30},{36,34... | collective-permute-start | bytes 4325384 | tf_op jit(solution)/shard_map/ppermute | solution.py:755
  161.2 2.2 %copy-start.3 = (f32[1024,1024]{1,0:T(8,128)S(1)}, f32[1024,1024]{1,0:T(8,128)}, u32[]{:S(2)}) copy-start(f32[1024,1024]{1,0:T(8,128)} %copy-done.2) | copy-start | bytes 12582916
  163.4 21.0 %copy-start.14 = (f32[64,64]{1,0:T(8,128)S(1)}, f32[64,64]{1,0:T(8,128)}, u32[]{:S(2)}) copy-start(f32[64,64]{1,0:T(8,128)} %param.7) | copy-start | bytes 49156
  183.7 1.2 copy-start.7
  184.9 14.4 %copy-start.4 = (f32[1408,256]{1,0:T(8,128)S(1)}, f32[1408,256]{1,0:T(8,128)}, u32[]{:S(2)}) copy-start(f32[1408,256]{1,0:T(8,128)} %second_products.1.kept_ref) | copy-start | bytes 4325380
  199.3 7.8 %copy-start.12 = (s32[3]{0:T(128)S(1)}, s32[3]{0:T(128)}, u32[]{:S(2)}) copy-start(s32[3]{0:T(128)} %copy-done.10) | copy-start | bytes 40
Sparse Core Ops, SparseCore 0:
  9.7 25.2 all-gather.2
  105.6 18.5 all-gather.4
where the time goes:
time: 217 us; the launch traced here: 216 us
  Pallas kernels  184 us (85%)
  between operations  14.3 us (7%)
  local copies, waits for them, and re-layouts  12.6 us (6%)
  starting transfers between devices  2.83 us (1%)
    pallas_call x1, Pallas kernels, on_device(): remote_call(pair_kernel, 'products_and_swap', 2, 58, out_shape=[shape_of(...  52.9 us
    pallas_call x1, Pallas kernels, inverse_of_packed(): local_call(packed_inverse_kernel, 'second_inverse', 24 * order ** 3, 20,...  34.1 us
    pallas_call x1, Pallas kernels, inverse_and_log(): local_call(inverse_kernel, 'first_inverse', 24 * order ** 3, 16, out_shap...  33.8 us
    pallas_call x1, Pallas kernels, on_device(): remote_call(functools.partial(reduce_kernel, SIDE), 'reduce_terms', 3, ou...  17.9 us
    pallas_call x1, Pallas kernels, on_device(): local_call(second_fill_kernel, 'second_fill', 6 * order ** 3, 58, out_sha...  14.3 us
    pallas_call x1, Pallas kernels, on_device(): local_call(second_products_kernel, 'second_products', 5 * order ** 3, 58,...  13.8 us
    unnamed x30, local copies, waits for them, and re-layouts  11.6 us
    pallas_call x1, Pallas kernels, on_device(): remote_call(finish_kernel, 'finish_blocks', 4, out_shape=[packed_shape, s...  7.04 us
  transfers between devices with their start and end apart: 4, of which 0 were waited for; matrix products, arithmetic and copies ran while one was open for 1% of the time, Pallas kernels for 56%

commit v1 on v0

--- a/solution.py
+++ b/solution.py
@@ -314,17 +314,17 @@
     last = slice(PACKED * BLOCK, None)
     copies = fetch(
         (
+            (left_hbm, left_ref),
             (inverse_hbm, inverse_ref),
-            (left_hbm, left_ref),
             (both_hbm.at[:, pl.ds(PACKED * BLOCK, arrow_ref.shape[1]), :], arrow_ref),
             (rest_hbm, rest_ref),
         ),
         sems,
     )
     copies[0].wait()
+    split_rows(left_ref, bh, bl)
+    copies[1].wait()
     split_rows(inverse_ref, vh, vl, -1)
-    copies[1].wait()
-    split_rows(left_ref, bh, bl)
     for copy in copies[2:]:
         copy.wait()
     rows = split_two(separator_arrow(arrow_ref[...]))
@@ -352,43 +352,42 @@
         out_ref[last, :] = rest_ref[last, :] - change
 
 
-def second_terms_kernel(info_ref, inverse_hbm, arrow_ref, pair_sums_ref, log_ref, sums_ref, inverse_ref, sem):
+def second_terms_kernel(
+    info_ref, inverse_hbm, pair_hbm, arrow_ref, pair_sums_ref, log_ref, sums_ref, xh_ref, xl_ref,
+    inverse_ref, pair_ref, sems, vh, vl,
+):
     sums_ref[...] = pair_sums_ref[...]
 
     @pl.when(info_ref[1] == 0)
     def _():
-        copy = pltpu.make_async_copy(inverse_hbm, inverse_ref, sem)
+        copies = fetch(((inverse_hbm, inverse_ref), (pair_hbm, pair_ref)), sems)
+        copies[0].wait()
+        put_sums(sums_ref, arrow_form(separator_arrow(arrow_ref[...]), inverse_ref), log_ref[...])
+        sums_ref[...] = sums_ref[...] + pair_sums_ref[...]
+        split_rows(inverse_ref, vh, vl, -1)
+        copies[1].wait()
+        solve_into((vh, vl), split_two(pair_ref[...]), (xh_ref, xl_ref), 0)
+
+
+def second_fill_kernel(info_ref, totals_ref, left_hbm, own_hbm, xh_ref, xl_ref, out_ref, left_ref, sem, bh, bl):
+    even = info_ref[1] == 1
+
+    @pl.when(even)
+    def _():
+        copy = pltpu.make_async_copy(own_hbm, out_ref.at[0], sem)
         copy.start()
         copy.wait()
-        put_sums(sums_ref, arrow_form(separator_arrow(arrow_ref[...]), inverse_ref), log_ref[...])
-        sums_ref[...] = sums_ref[...] + pair_sums_ref[...]
-
-
-def second_fill_kernel(
-    info_ref, totals_ref, inverse_hbm, left_hbm, own_hbm, pair_hbm, out_ref,
-    inverse_ref, left_ref, pair_ref, sems, vh, vl, bh, bl, xh, xl,
-):
-    even = info_ref[1] == 1
-
-    @pl.when(even)
-    def _():
-        copy = pltpu.make_async_copy(own_hbm, out_ref.at[0], sems.at[0])
+
+    @pl.when(jnp.logical_not(even))
+    def _():
+        copy = pltpu.make_async_copy(left_hbm, left_ref, sem)
         copy.start()
         copy.wait()
-
-    @pl.when(jnp.logical_not(even))
-    def _():
-        copies = fetch(((inverse_hbm, inverse_ref), (pair_hbm, pair_ref), (left_hbm, left_ref)), sems)
-        copies[0].wait()
-        split_rows(inverse_ref, vh, vl, -1)
-        copies[1].wait()
-        solve_into((vh, vl), split_two(pair_ref[...]), (xh, xl), 0)
-        copies[2].wait()
         split_rows(left_ref, bh, bl)
 
         def part(r, carry):
             rows = block_span(r)
-            out_ref[0, rows, :] = -times((bh[rows, :], bl[rows, :]), (xh[...], xl[...]))
+            out_ref[0, rows, :] = -times((bh[rows, :], bl[rows, :]), (xh_ref[...], xl_ref[...]))
             return carry
 
         lax.fori_loop(0, bh.shape[0] // BLOCK, part, 0)
@@ -460,8 +459,8 @@
     own = pl.ds(pl.multiple_of(core * half, half), half)
     copies = fetch(
         (
+            (sub_hbm.at[0], left_ref),
             (inverse_hbm, inverse_ref),
-            (sub_hbm.at[0], left_ref),
             (sub_hbm.at[1], right_ref),
             (diag_hbm.at[1], diag_ref),
             (own_arrow_hbm.at[1], own_arrow_ref),
@@ -469,9 +468,9 @@
         sems,
     )
     copies[0].wait()
+    split_rows(left_ref, bh, bl)
+    copies[1].wait()
     split_rows(inverse_ref, vh, vl, -1)
-    copies[1].wait()
-    split_rows(left_ref, bh, bl)
     solve_into((vh, vl), (bh[:, own], bl[:, own]), (xh, xl), 0)
     copies[2].wait()
     split_rows(right_ref, sh, sl)
@@ -753,13 +752,13 @@
         + thin,
     )(info, inverse, left_full, both, rest)
     above = lax.ppermute(product, "tm", down)
-    sums = local_call(
-        second_terms_kernel, "second_terms", order**3 // 2, 24,
-        out_shape=shape_of(effects + 8, TILE),
-        in_specs=[SMEM_SPEC, ANY_SPEC, *vmem(3)],
-        out_specs=vmem(1)[0],
-        scratch_shapes=[pltpu.VMEM(square, F32), pltpu.SemaphoreType.DMA],
-    )(info, inverse, both[:, PACKED * BLOCK :], pair_sums, log_second)
+    sums, x_high, x_low = local_call(
+        second_terms_kernel, "second_terms", 3 * order**3, 58,
+        out_shape=[shape_of(effects + 8, TILE)] + [shape_of(*tall, dtype=BF16)] * 2,
+        in_specs=[SMEM_SPEC, *[ANY_SPEC] * 2, *vmem(3)],
+        out_specs=vmem(3),
+        scratch_shapes=[pltpu.VMEM(square, F32), pltpu.VMEM(tall, F32), dma_sems(2)] + big,
+    )(info, inverse, left_pair, both[:, PACKED * BLOCK :], pair_sums, log_second)
     totals = remote_call(
         functools.partial(reduce_kernel, SIDE), "reduce_terms", 3,
         out_shape=shape_of(effects + 8, TILE), in_specs=vmem(1), out_specs=vmem(1)[0],
@@ -769,12 +768,12 @@
         ],
     )(sums)
     left_result = local_call(
-        second_fill_kernel, "second_fill", 6 * order**3, 58,
+        second_fill_kernel, "second_fill", 3 * order**3, 58,
         out_shape=shape_of(1, *tall),
-        in_specs=[SMEM_SPEC, *vmem(1), *[ANY_SPEC] * 4],
+        in_specs=[SMEM_SPEC, *vmem(1), *[ANY_SPEC] * 2, *vmem(2)],
         out_specs=vmem(1)[0],
-        scratch_shapes=[pltpu.VMEM(square, F32)] * 2 + [pltpu.VMEM(tall, F32), dma_sems(3)] + big * 2 + thin,
-    )(info, totals, inverse, left_full, left_own, left_pair)
+        scratch_shapes=[pltpu.VMEM(square, F32), pltpu.SemaphoreType.DMA] + big,
+    )(info, totals, left_full, left_own, x_high, x_low)
     packed, swapped = remote_call(
         finish_kernel, "finish_blocks", 4,
         out_shape=[packed_shape, shape_of(2 * BLOCK, BLOCK)], in_specs=vmem(2), out_specs=vmem(2),

time: 217 us -> 219 us (level)
  Pallas kernels: 184 us -> 187 us
    pallas_call x2, Pallas kernels: 16.7 us -> 21.2 us  [the longest x1 11.4 us: on_device(): local_call(second_terms_kernel, 'second_terms', 3 * order ** 3, 58, out_s...]
  transfers between devices with their start and end apart: 4 -> 4, of which waited for: 0 -> 0; matrix products, arithmetic and copies ran while one was open for 1% -> 1% of each run, Pallas kernels for 56% -> 57%
where the time goes in v1:
time: 219 us
  Pallas kernels  187 us (85%)
  between operations  14.3 us (7%)
  local copies, waits for them, and re-layouts  12.5 us (6%)
  starting transfers between devices  2.83 us (1%)
    pallas_call x1, Pallas kernels, on_device(): remote_call(pair_kernel, 'products_and_swap', 2, 58, out_shape=[shape_of(...  53 us
    pallas_call x1, Pallas kernels, inverse_of_packed(): local_call(packed_inverse_kernel, 'second_inverse', 24 * order ** 3, 20,...  34.1 us
    pallas_call x1, Pallas kernels, inverse_and_log(): local_call(inverse_kernel, 'first_inverse', 24 * order ** 3, 16, out_shap...  33.8 us
    pallas_call x1, Pallas kernels, on_device(): remote_call(functools.partial(reduce_kernel, SIDE), 'reduce_terms', 3, ou...  17.7 us
    pallas_call x1, Pallas kernels, on_device(): local_call(second_products_kernel, 'second_products', 5 * order ** 3, 58,...  13.7 us
    pallas_call x1, Pallas kernels, on_device(): local_call(second_terms_kernel, 'second_terms', 3 * order ** 3, 58, out_s...  11.4 us
    unnamed x30, local copies, waits for them, and re-layouts  10.8 us
    pallas_call x1, Pallas kernels, on_device(): local_call(second_fill_kernel, 'second_fill', 3 * order ** 3, 58, out_sha...  9.84 us
  transfers between devices with their start and end apart: 4, of which 0 were waited for; matrix products, arithmetic and copies ran while one was open for 1% of the time, Pallas kernels for 57%

profile of v1, /device:TPU:25, one launch (start us, length us, event | category | flops | bytes accessed | tf_op | source)
XLA Modules:
  0.0 218.8 jit_solution(5335032470467586841)
XLA Ops:
  7.2 0.7 all-gather.3.cloned.1.call-update
  8.1 2.2 copy-done
  10.3 5.2 %gather_pivot.1 = (f32[1024,1024]{1,0:T(8,128)S(1)}, f32[1,64,1024]{2,1,0:T(8,128)S(1)}) custom-call(f32[2,1024,512]{2,1,0:T(8,128)S(1)} %copy-done, f32[2,64,512]{2,1,0:T(8,128)S(1)} %copy-done.3), custom_call_target="tpu_custom_call" | custom-call | tf_op jit(solution)/shard_map/gather_pivot/pallas_call | solution.py:715
  15.5 0.7 copy-done.4
  16.2 33.8 %first_inverse.1 = (f32[1024,1024]{1,0:T(8,128)S(1)}, f32[8,128]{1,0:T(8,128)S(1)}) custom-call(f32[1024,1024]{1,0:T(8,128)S(1)} %get-tuple-element.21.source_ref), custom_call_target="tpu_custom_call" | custom-call | flops 25769803776 | bytes 8388608 | tf_op jit(solution)/shard_map/first_inverse/pallas_call | solution.py:213
  50.0 2.0 copy-done.1
  51.9 0.6 copy-done.8
  52.5 53.0 %products_and_swap.1 = (f32[2,1408,256]{2,1,0:T(8,128)}, f32[1024,512]{1,0:T(8,128)}, f32[1408,256]{1,0:T(8,128)}, f32[72,128]{1,0:T(8,128)}) custom-call(f32[1024,1024]{1,0:T(8,128)} %copy-done.1, f32[2,1024,1024]{2,1,0:T(8,128)} %all-gather.3.cloned.1.call-done.sub_hbm, f32[2,1024,512]{2,1,0:T(8,128)} %diag_hbm.1, f32[2,64,512]{2,1,0:T(8,128)} %own_arrow_hbm.1, ...), custom_call_target="tpu_custom_call" | custom-call | tf_op jit(solution)/shard_map/products_and_swap/pallas_call | solution.py:727
  105.6 1.5 collective-permute-start.1
  107.1 1.8 copy-done.7
  108.9 34.1 %second_inverse.1 = (f32[1024,1024]{1,0:T(8,128)S(1)}, f32[8,128]{1,0:T(8,128)S(1)}, f32[1024,512]{1,0:T(8,128)S(1)}) custom-call(s32[3]{0:T(128)S(1)} %pad_add_fusion.info_ref, f32[2,1408,256]{2,1,0:T(8,128)S(1)} %copy-done.7), custom_call_target="tpu_custom_call" | custom-call | flops 25769803776 | bytes 8388608 | tf_op jit(solution)/shard_map/second_inverse/pallas_call | solution.py:221
  143.1 2.0 copy-done.11
  145.7 13.7 %second_products.1.kept_ref = f32[1408,256]{1,0:T(8,128)} custom-call(s32[3]{0:T(128)} %copy-done.9, f32[1024,1024]{1,0:T(8,128)} %copy-done.11, f32[1024,1024]{1,0:T(8,128)} %all-gather.5.cloned.1.call-done.left_hbm, f32[2,1408,256]{2,1,0:T(8,128)} %get-tuple-element.25.both_ref.both_hbm, f32[1408,256]{1,0:T(8,128)} %get-tuple-element.28.rest_hbm), custom_call_target="tpu_custom_call" | custom-call | flops 5368709120 | bytes 8388608 | tf_op jit(solution)/shard_map/second_products/pallas_call | solution.py:744
  159.4 1.3 collective-permute-start
  160.7 1.7 slice.19.arrow_ref
  162.4 11.4 %second_terms.1 = (f32[72,128]{1,0:T(8,128)}, bf16[1024,512]{1,0:T(8,128)(2,1)}, bf16[1024,512]{1,0:T(8,128)(2,1)}) custom-call(s32[3]{0:T(128)} %copy-done.9, f32[1024,1024]{1,0:T(8,128)} %copy-done.11, f32[1024,512]{1,0:T(8,128)} %collective-permute-done.1.pair_hbm, f32[2,128,256]{2,1,0:T(8,128)} %slice.19.arrow_ref, ...), custom_call_target="tpu_custom_call" | custom-call | flops 3221225472 | bytes 8388608 | tf_op jit(solution)/shard_map/second_terms/pallas_call | solution.py:755
  173.8 0.8 copy-done.6
  174.6 17.7 %reduce_terms.1.totals_ref = f32[72,128]{1,0:T(8,128)S(1)} custom-call(f32[72,128]{1,0:T(8,128)S(1)} %copy-done.6), custom_call_target="tpu_custom_call" | custom-call | tf_op jit(solution)/shard_map/reduce_terms/pallas_call | solution.py:762
  192.3 0.6 slice_reduce_fusion
  192.9 0.6 slice_subtract_fusion
  193.5 9.8 %second_fill.1 = f32[1,1024,512]{2,1,0:T(8,128)} custom-call(s32[3]{0:T(128)} %copy-done.9, f32[72,128]{1,0:T(8,128)} %copy-done.5, f32[1024,1024]{1,0:T(8,128)} %all-gather.5.cloned.1.call-done.left_hbm, f32[1024,512]{1,0:T(8,128)} %get-tuple-element.27.own_hbm, bf16[1024,512]{1,0:T(8,128)(2,1)} %get-tuple-element.35.xh_ref, ...), custom_call_target="tpu_custom_call" | custom-call | flops 3221225472 | bytes 8388608 | tf_op jit(solution)/shard_map/second_fill/pallas_call | solution.py:770
  203.4 5.6 %finish_blocks.1 = (f32[1408,256]{1,0:T(8,128)S(1)}, f32[512,256]{1,0:T(8,128)S(1)}) custom-call(f32[1408,256]{1,0:T(8,128)S(1)} %copy-done.2, f32[1408,256]{1,0:T(8,128)S(1)} %collective-permute-done.above_ref), custom_call_target="tpu_custom_call" | custom-call | tf_op jit(solution)/shard_map/finish_blocks/pallas_call | solution.py:777
  209.1 0.7 maximum_bitcast_fusion
  209.8 2.2 place_blocks.1
  (33 shorter events, 1.0 us)
Async XLA Ops:
  7.2 1.0 copy-start.3
  7.2 45.4 %all-gather.3.cloned.1.call-start = ((), (), s32[]{:S(2)}) async-start(), calls=%async_computation | async-start | bytes 12582912 | tf_op jit(solution)/shard_map/all_gather | solution.py:721
  7.9 137.8 %all-gather.5.cloned.1.call-start = ((), (), s32[]{:S(2)}) async-start(), calls=%async_computation.1 | async-start | bytes 6291456 | tf_op jit(solution)/shard_map/all_gather | solution.py:741
  8.1 2.2 copy-start
  15.5 0.7 copy-start.4
  50.0 2.0 copy-start.1
  51.9 0.6 copy-start.8
  105.6 37.4 %copy-start.9 = (s32[3]{0:T(128)}, s32[3]{0:T(128)S(1)}, u32[]{:S(2)}) copy-start(s32[3]{0:T(128)S(1)} %pad_add_fusion.info_ref) | copy-start | bytes 40
  105.6 56.8 %collective-permute-start.1 = (f32[1024,512]{1,0:T(8,128)}, f32[1024,512]{1,0:T(8,128)}, u32[]{:S(2)}, u32[]{:S(2)}) collective-permute-start(f32[1024,512]{1,0:T(8,128)} %get-tuple-element.27.own_hbm), channel_id=1, source_target_pairs={{0,2},{4,6},{8,10},{12,14},{16,18},{20,22},{24,26},{28,30},{32,34}... | collective-permute-start | bytes 6291464 | tf_op jit(solution)/shard_map/ppermute | solution.py:740
  107.1 1.8 copy-start.7
  143.1 2.0 copy-start.11
  145.1 0.6 copy-start.12
  159.4 44.0 %collective-permute-start = (f32[1408,256]{1,0:T(8,128)}, f32[1408,256]{1,0:T(8,128)S(1)}, u32[]{:S(2)}, u32[]{:S(2)}) collective-permute-start(f32[1408,256]{1,0:T(8,128)} %second_products.1.kept_ref), channel_id=1, source_target_pairs={{4,2},{8,6},{12,10},{16,14},{20,18},{24,22},{28,26},{32,30},{36,34... | collective-permute-start | bytes 4325384 | tf_op jit(solution)/shard_map/ppermute | solution.py:754
  162.4 30.5 %copy-start.14 = (f32[64,64]{1,0:T(8,128)S(1)}, f32[64,64]{1,0:T(8,128)}, u32[]{:S(2)}) copy-start(f32[64,64]{1,0:T(8,128)} %param.7) | copy-start | bytes 49156
  173.8 0.8 copy-start.6
  192.3 1.2 copy-start.5
  193.5 9.9 %copy-start.2 = (f32[1408,256]{1,0:T(8,128)S(1)}, f32[1408,256]{1,0:T(8,128)}, u32[]{:S(2)}) copy-start(f32[1408,256]{1,0:T(8,128)} %second_products.1.kept_ref) | copy-start | bytes 4325380
  203.4 5.7 %copy-start.13 = (f32[2,128,256]{2,1,0:T(8,128)S(1)}, f32[2,128,256]{2,1,0:T(8,128)}, u32[]{:S(2)}) copy-start(f32[2,128,256]{2,1,0:T(8,128)} %slice.19.arrow_ref) | copy-start | bytes 786436
  203.4 6.4 %copy-start.10 = (s32[3]{0:T(128)S(1)}, s32[3]{0:T(128)}, u32[]{:S(2)}) copy-start(s32[3]{0:T(128)} %copy-done.9) | copy-start | bytes 40
Sparse Core Ops, SparseCore 0:
  9.7 25.2 all-gather.2
  105.7 18.5 all-gather.4
